TPU v7x, 32 devices: a whole 2x2x4 slice. The times are simulated.
32 devices in a mesh: groups: 2 (over x), pool: 8 (over z, y), head: 2 (over core).
Axes of the slice: x: 2, y: 2, z: 4, core: 2. Of those that a mesh axis runs over, the one named last changes fastest.
Arguments:
- queries: bfloat16 [2048, 32, 128], P(('groups', 'pool'), 'head'), parts along dimension 0, may hold values from -400 to 400
- new_kv: bfloat16 [2048, 2, 4, 128], P(('groups', 'pool'), None, 'head'), parts along dimension 0, may hold values from -4 to 4
- pool: bfloat16 [528, 2, 4, 128, 128], P(('groups', 'pool'), None, 'head'), parts along dimension 0, may hold values from -6 to 6
- block_table: int32 [8, 64], P('groups'), parts along dimension 0, may hold values from -1 to 263, as said below
- prefix_len: int32 [8], P('groups'), parts along dimension 0, may hold values from 2048 to 8192, as said below
- new_slots: int32 [16], P('groups'), parts along dimension 0, may hold values from 0 to 263, as said below
Outputs:
- attended: bfloat16 [2048, 32, 128], P(('groups', 'pool'), 'head'), parts along dimension 0
- updated_pool: bfloat16 [528, 2, 4, 128, 128], P(('groups', 'pool'), None, 'head'), parts along dimension 0
There are 2 independent parts, one for each index of `groups`. A program takes and returns all parts, laid end to end along the dimension named above; each array names one. Nothing has to cross between parts.
Inputs may be any that keep to these rules, and one draw needn't show every extreme that they name: `block_table`: entry [r, j] is the slot (owner times 33 plus local slot) of page j of request r for j < ceil(prefix_len[r] / 128), and -1 after. All named slots differ. No owner holds more than 8 pages of one request, and the request with the longest prefix has exactly 8 on every owner. `prefix_len`: the longest prefix is exactly 8192 tokens. `new_slots`: entry d is a slot of owner d (d * 33 to (d + 1) * 33 - 1) that block_table does not name.
All inputs are finite; a program needn't handle non-finite values.
Results may differ from a plain program's by a relative error of at most 0.012.
Values may be sent and summed in bfloat16 or wider, within the bound.
A program may use at most 128 MiB of HBM per device.

v0:
```python
import jax
import jax.numpy as jnp
from jax import lax
from jax.sharding import PartitionSpec as P

neg_big = -1e30
pages_per_step = 8


def swapped(array, axis, apart):
    return lax.ppermute(array, axis, [(i, i ^ 1 << apart) for i in range(lax.axis_size(axis))])


def select_pages(block_rows, lengths, holder, first_rank, take_count, slot_count, page_len):
    column = jnp.arange(block_rows.shape[1], dtype=jnp.int32)
    page_count = (lengths + page_len - 1) // page_len
    owned = (
        (block_rows // slot_count == holder[:, None])
        & (column[None, :] < page_count[:, None])
        & (block_rows >= 0)
    )
    order_rank = jnp.cumsum(owned.astype(jnp.int32), axis=1) - 1
    wanted = first_rank[:, None] + jnp.arange(take_count, dtype=jnp.int32)[None, :]
    matched = owned[:, None, :] & (order_rank[:, None, :] == wanted[:, :, None])
    present = jnp.any(matched, axis=-1)
    chosen = jnp.sum(jnp.where(matched, column[None, None, :], 0), axis=-1)
    slot_id = jnp.sum(jnp.where(matched, (block_rows % slot_count)[:, None, :], 0), axis=-1)
    return (chosen, slot_id, present)


def prepare(
    pool, block_table, prefix_len, owner_id, request_id, take_count, send_first, recv_first
):
    owner_count = lax.axis_size("pool")
    slot_count = pool.shape[0]
    page_len = pool.shape[3]
    targets = jnp.arange(owner_count, dtype=jnp.int32)
    send_rows = block_table[targets // 2]
    send_lengths = prefix_len[targets // 2]
    holder_self = jnp.full((owner_count,), owner_id, jnp.int32)
    unused, send_slots, unused_present = select_pages(
        send_rows, send_lengths, holder_self, send_first, take_count, slot_count, page_len
    )
    buffer = pool[send_slots]
    recv_rows = jnp.broadcast_to(block_table[request_id][None, :], send_rows.shape)
    recv_lengths = jnp.broadcast_to(prefix_len[request_id], (owner_count,))
    chosen, unused_slots, present = select_pages(
        recv_rows, recv_lengths, targets, recv_first, take_count, slot_count, page_len
    )
    position = chosen[..., None] * page_len + jnp.arange(page_len, dtype=jnp.int32)
    mask_in = (present[..., None] & (position < prefix_len[request_id])).reshape(-1, page_len)
    return (buffer, mask_in)


def update(running, scores, allowed, carry_values):
    top_old, total_old, acc_old = running
    scores = jnp.where(allowed, scores, neg_big)
    top_new = jnp.maximum(top_old, jnp.max(scores, axis=-1))
    weights = jnp.where(allowed, jnp.exp(scores - top_new[..., None]), 0.0)
    factor = jnp.exp(top_old - top_new)
    total_new = total_old * factor + jnp.sum(weights, axis=-1)
    acc_new = acc_old * factor[..., None] + carry_values(weights.astype(jnp.bfloat16))
    return (top_new, total_new, acc_new)


def attend(query_rows, pages_in, mask_in, recent_kv, recent_allowed, kv_heads, group_size):
    n_rows = query_rows.shape[0]
    head_dim = query_rows.shape[2]
    page_len = pages_in.shape[-2]
    scale = head_dim ** (-0.5)
    query_heads = query_rows.reshape(n_rows, kv_heads, group_size, head_dim)
    running = (
        jnp.full((kv_heads, group_size, n_rows), neg_big, jnp.float32),
        jnp.zeros((kv_heads, group_size, n_rows), jnp.float32),
        jnp.zeros((kv_heads, group_size, n_rows, head_dim), jnp.float32),
    )
    recent_scores = (
        jnp.einsum(
            "tkgd,ckd->kgtc", query_heads, recent_kv[:, 0], preferred_element_type=jnp.float32
        )
        * scale
    )

    def recent_values(probs):
        return jnp.einsum(
            "kgtc,ckd->kgtd", probs, recent_kv[:, 1], preferred_element_type=jnp.float32
        )

    running = update(running, recent_scores, recent_allowed[None, None], recent_values)

    def turn(turn_index, running):
        begin = turn_index * pages_per_step
        page_block = lax.dynamic_slice_in_dim(pages_in, begin, pages_per_step, 0)
        block_mask = lax.dynamic_slice_in_dim(mask_in, begin, pages_per_step, 0)
        scores = jnp.einsum(
            "tkgd,nkpd->kgtnp", query_heads, page_block[:, 0], preferred_element_type=jnp.float32
        )
        scores = scores.reshape(kv_heads, group_size, n_rows, pages_per_step * page_len) * scale

        def carry_values(probs):
            shaped = probs.reshape(kv_heads, group_size, n_rows, pages_per_step, page_len)
            return jnp.einsum(
                "kgtnp,nkpd->kgtd", shaped, page_block[:, 1], preferred_element_type=jnp.float32
            )

        return update(running, scores, block_mask.reshape(1, 1, 1, -1), carry_values)

    return lax.fori_loop(0, pages_in.shape[0] // pages_per_step, turn, running)


def half_of(device_ids):
    return 1 - (device_ids % 2 ^ device_ids // 2 % 2)


def on_device(queries, new_kv, pool, block_table, prefix_len, new_slots):
    owner_count = lax.axis_size("pool")
    owner_id = lax.axis_index("pool")
    request_id = owner_id // 2
    pair_half = half_of(owner_id)
    slot_count = pool.shape[0]
    kv_heads = pool.shape[2]
    page_len = pool.shape[3]
    head_dim = pool.shape[4]
    tok_rows = queries.shape[0]
    q_heads = queries.shape[1]
    group_size = q_heads // kv_heads
    page_cap = block_table.shape[1] // owner_count
    targets = jnp.arange(owner_count, dtype=jnp.int32)
    recent_pos = jnp.arange(2 * tok_rows, dtype=jnp.int32)
    half_cap = page_cap // 2
    send_first = half_of(targets) * half_cap
    recv_first = jnp.full((owner_count,), pair_half * half_cap, jnp.int32)
    buffer, mask_in = prepare(
        pool, block_table, prefix_len, owner_id, request_id, half_cap, send_first, recv_first
    )
    pages_in = lax.all_to_all(buffer, "pool", split_axis=0, concat_axis=0, tiled=True)
    pages_in = pages_in.reshape(-1, 2, kv_heads, page_len, head_dim)
    partner_q, partner = swapped((queries, new_kv), "pool", 0)
    recent_kv = jnp.where(
        pair_half == 0,
        jnp.concatenate([new_kv, partner], axis=0),
        jnp.concatenate([partner, new_kv], axis=0),
    )
    query_rows = jnp.where(
        pair_half == 0,
        jnp.concatenate([queries, partner_q], axis=0),
        jnp.concatenate([partner_q, queries], axis=0),
    )
    recent_allowed = (recent_pos[None, :] <= recent_pos[:, None]) & (pair_half == 0)
    running = attend(query_rows, pages_in, mask_in, recent_kv, recent_allowed, kv_heads, group_size)
    own_start = pair_half * tok_rows
    other_start = (1 - pair_half) * tok_rows
    own_part = tuple((lax.dynamic_slice_in_dim(piece, own_start, tok_rows, 2) for piece in running))
    theirs = tuple((lax.dynamic_slice_in_dim(piece, other_start, tok_rows, 2) for piece in running))
    returned = (
        swapped(theirs[0].astype(jnp.bfloat16), "pool", 0).astype(jnp.float32),
        swapped(theirs[1].astype(jnp.bfloat16), "pool", 0).astype(jnp.float32),
        swapped(theirs[2].astype(jnp.bfloat16), "pool", 0).astype(jnp.float32),
    )
    top_new = jnp.maximum(own_part[0], returned[0])
    factor_own = jnp.exp(own_part[0] - top_new)
    factor_back = jnp.exp(returned[0] - top_new)
    total_new = own_part[1] * factor_own + returned[1] * factor_back
    acc_new = own_part[2] * factor_own[..., None] + returned[2] * factor_back[..., None]
    combined = (top_new, total_new, acc_new)
    mixed = combined[2] / combined[1][..., None]
    attended = mixed.transpose(2, 0, 1, 3).reshape(tok_rows, q_heads, head_dim).astype(jnp.bfloat16)
    new_page = new_kv.transpose(1, 2, 0, 3)[None]
    own_slot = lax.dynamic_index_in_dim(new_slots, owner_id, 0, keepdims=False)
    slot_id = own_slot % slot_count
    updated_pool = lax.dynamic_update_slice_in_dim(pool, new_page, slot_id, 0)
    return (attended, updated_pool)


def solution(mesh):
    placed = (
        P(("groups", "pool"), "head", None),
        P(("groups", "pool"), None, "head", None),
        P(("groups", "pool"), None, "head", None, None),
        P("groups", None),
        P("groups"),
        P("groups"),
    )
    return jax.shard_map(
        on_device,
        mesh=mesh,
        in_specs=placed,
        out_specs=(
            P(("groups", "pool"), "head", None),
            P(("groups", "pool"), None, "head", None, None),
        ),
        check_vma=False,
    )
```

profile of v0, /device:TPU:2, one launch (start us, length us, event | category | flops | bytes accessed | tf_op | source)
XLA Modules:
  0.0 198.3 jit_solution(16582899362481627354)
XLA Ops:
  0.7 5.9 %copy.109 = bf16[33,2,2,128,128]{4,3,2,1,0:T(8,128)(2,1)} copy(bf16[33,2,2,128,128]{4,3,2,1,0:T(8,128)(2,1)} %param.10) | data formatting | bytes 8650752
  8.6 5.2 %gather_fusion.2 = bf16[32,2,2,128,128]{4,3,2,1,0:T(8,128)(2,1)} fusion(bf16[33,2,2,128,128]{4,3,2,1,0:T(8,128)(2,1)} %copy.109, s32[1024]{0:T(1024)S(1)} %pad_clamp_fusion), kind=kCustom, calls=%fused_computation.2 | custom fusion | bytes 8388736 | tf_op jit(solution)/shard_map/gather | solution.py:44
  13.8 4.7 %copy.63 = bf16[8,4,2,2,128,128]{5,4,1,3,2,0:T(8,128)(2,1)} copy(bf16[8,4,2,2,128,128]{5,4,3,2,1,0:T(8,128)(2,1)} %bitcast.113) | data formatting | bytes 8388608 | tf_op jit(solution)/shard_map/gather | solution.py:44
  18.6 6.0 %all-to-all-start = ((bf16[8,4,2,2,128,128]{5,4,1,3,2,0:T(8,128)(2,1)}), bf16[8,4,2,2,128,128]{5,4,1,3,2,0:T(8,128)(2,1)}, u32[]{:S(2)}, u32[]{:S(2)}) async-start(bf16[8,4,2,2,128,128]{5,4,1,3,2,0:T(8,128)(2,1)} %copy.63), calls=%async_computation | async-start | bytes 8388608 | tf_op jit(solution)/shard_map/all_to_all | solution.py:136
  24.6 2.1 %collective-permute-start = (bf16[128,2,2,128]{3,0,2,1:T(8,128)(2,1)S(1)}, bf16[128,2,2,128]{3,0,2,1:T(8,128)(2,1)S(1)}, u32[]{:S(2)}, u32[]{:S(2)}) collective-permute-start(bf16[128,2,2,128]{3,0,2,1:T(8,128)(2,1)S(1)} %copy.55), channel_id=1, source_target_pairs={{0,2},{2,0},{4,6},{6,4},{8,10},{10,8},{12,14},{14,12},{1,3},{3,1},... | collective-permute-start | bytes 393224 | tf_op jit(solution)/shard_map/ppermute | solution.py:11
  31.2 32.3 %collective-permute-done = bf16[128,2,2,128]{3,0,2,1:T(8,128)(2,1)S(1)} collective-permute-done((bf16[128,2,2,128]{3,0,2,1:T(8,128)(2,1)S(1)}, bf16[128,2,2,128]{3,0,2,1:T(8,128)(2,1)S(1)}, u32[]{:S(2)}, u32[]{:S(2)}) %collective-permute-start) | collective-permute-done | bytes 131104 | tf_op jit(solution)/shard_map/ppermute | solution.py:11
  63.5 12.5 %collective-permute-done.1 = bf16[128,16,128]{2,1,0:T(8,128)(2,1)S(1)} collective-permute-done((bf16[128,16,128]{2,1,0:T(8,128)(2,1)S(1)}, bf16[128,16,128]{2,1,0:T(8,128)(2,1)S(1)}, u32[]{:S(2)}, u32[]{:S(2)}) %collective-permute-start.1) | collective-permute-done | bytes 524320 | tf_op jit(solution)/shard_map/ppermute | solution.py:11
  78.3 1.7 fusion.27
  80.0 37.8 %all-to-all-done = bf16[8,4,2,2,128,128]{5,4,1,3,2,0:T(8,128)(2,1)} async-done(((bf16[8,4,2,2,128,128]{5,4,1,3,2,0:T(8,128)(2,1)}), bf16[8,4,2,2,128,128]{5,4,1,3,2,0:T(8,128)(2,1)}, u32[]{:S(2)}, u32[]{:S(2)}) %all-to-all-start) | async-done | bytes 4194336 | tf_op jit(solution)/shard_map/all_to_all | solution.py:136
  117.8 4.7 %copy.64 = bf16[8,4,2,2,128,128]{5,4,3,2,1,0:T(8,128)(2,1)} copy(bf16[8,4,2,2,128,128]{5,4,1,3,2,0:T(8,128)(2,1)} %all-to-all-done) | data formatting | bytes 8388608 | tf_op jit(solution)/shard_map/all_to_all | solution.py:136
  122.5 59.1 %while.17 = (s32[]{:T(128)}, f32[2,8,256]{2,1,0:T(8,128)S(1)}, f32[2,8,256]{2,1,0:T(8,128)S(1)}, f32[2,8,256,128]{3,2,1,0:T(8,128)S(1)}, pred[32,128]{1,0:T(8,12...) while((s32[]{:T(128)}, f32[2,8,256]{2,1,0:T(8,128)S(1)}, ...), condition=%wide.region_10.11_spmd, body=%wide.region_7.10_spmd.sunk | while | flops 2203066368 | bytes 58987704 | solution.py:108
  123.9 2.5 %bitcast_reduce_fusion.2 = (f32[2,8,256]{2,1,0:T(8,128)S(1)}, f32[2,8,128,256,8]{3,2,4,1,0:T(8,128)S(1)}) fusion(pred[8,128]{1,0:T(8,128)(4,1)S(1)} %constant_dynamic-slice_fusion.6, bf16[256,2,8,128]{3,0,2,1:T(8,128)(2,1)S(1)} %get-tuple-element.267, bf16[8,1,2,128,128]{4,3,2,1,0:T(8,128)(2,1)S(1)} %get-tuple-element.231), kind=kOutput, calls=%fused_computation.4.clone.1 | convolution fusion | flops 1086320640 | bytes 18367488 | tf_op jit(solution)/shard_map/while/body/eval_jaxpr/tkgd,nkpd->kgtnp/dot_general | solution.py:95
  126.4 4.4 %fusion.64 = f32[2,8,256]{2,1,0:T(8,128)S(1)} fusion(f32[2,8,128,256,8]{3,2,4,1,0:T(8,128)S(1)} %get-tuple-element.233, f32[2,8,256]{2,1,0:T(8,128)S(1)} %max.20, pred[8,128]{1,0:T(8,128)(4,1)S(1)} %constant_dynamic-slice_fusion.6), kind=kLoop, calls=%fused_computation.9.clone.1 | loop fusion | flops 20967424 | bytes 16811008 | tf_op jit(solution)/shard_map/while/body/eval_jaxpr/reduce_sum | solution.py:61
  130.9 6.4 %bitcast_add_fusion.2 = f32[2,8,256,128]{3,2,1,0:T(8,128)S(1)} fusion(f32[2,8,256,128]{3,2,1,0:T(8,128)S(1)} %get-tuple-element.252, f32[2,8,128,256,8]{3,2,4,1,0:T(8,128)S(1)} %get-tuple-element.233, f32[2,8,256]{2,1,0:T(8,128)S(1)} %max.20, pred[8,128]{1,0:T(8,128)(4,1)S(1)} %constant_dynamic-slice_fusion.6, ...), kind=kOutput, calls=%fused_computation.13.clone.1 | convolution fusion | flops 1095761920 | bytes 21529600 | tf_op jit(solution)/shard_map/while/body/eval_jaxpr/kgtnp,nkpd->kgtd/dot_general | solution.py:102
  138.6 2.5 %bitcast_reduce_fusion.2 = (f32[2,8,256]{2,1,0:T(8,128)S(1)}, f32[2,8,128,256,8]{3,2,4,1,0:T(8,128)S(1)}) fusion(pred[8,128]{1,0:T(8,128)(4,1)S(1)} %constant_dynamic-slice_fusion.6, bf16[256,2,8,128]{3,0,2,1:T(8,128)(2,1)S(1)} %get-tuple-element.267, bf16[8,1,2,128,128]{4,3,2,1,0:T(8,128)(2,1)S(1)} %get-tuple-element.231), kind=kOutput, calls=%fused_computation.4.clone.1 | convolution fusion | flops 1086320640 | bytes 18367488 | tf_op jit(solution)/shard_map/while/body/eval_jaxpr/tkgd,nkpd->kgtnp/dot_general | solution.py:95
  141.2 4.4 %fusion.64 = f32[2,8,256]{2,1,0:T(8,128)S(1)} fusion(f32[2,8,128,256,8]{3,2,4,1,0:T(8,128)S(1)} %get-tuple-element.233, f32[2,8,256]{2,1,0:T(8,128)S(1)} %max.20, pred[8,128]{1,0:T(8,128)(4,1)S(1)} %constant_dynamic-slice_fusion.6), kind=kLoop, calls=%fused_computation.9.clone.1 | loop fusion | flops 20967424 | bytes 16811008 | tf_op jit(solution)/shard_map/while/body/eval_jaxpr/reduce_sum | solution.py:61
  145.7 6.4 %bitcast_add_fusion.2 = f32[2,8,256,128]{3,2,1,0:T(8,128)S(1)} fusion(f32[2,8,256,128]{3,2,1,0:T(8,128)S(1)} %get-tuple-element.252, f32[2,8,128,256,8]{3,2,4,1,0:T(8,128)S(1)} %get-tuple-element.233, f32[2,8,256]{2,1,0:T(8,128)S(1)} %max.20, pred[8,128]{1,0:T(8,128)(4,1)S(1)} %constant_dynamic-slice_fusion.6, ...), kind=kOutput, calls=%fused_computation.13.clone.1 | convolution fusion | flops 1095761920 | bytes 21529600 | tf_op jit(solution)/shard_map/while/body/eval_jaxpr/kgtnp,nkpd->kgtd/dot_general | solution.py:102
  153.4 2.5 %bitcast_reduce_fusion.2 = (f32[2,8,256]{2,1,0:T(8,128)S(1)}, f32[2,8,128,256,8]{3,2,4,1,0:T(8,128)S(1)}) fusion(pred[8,128]{1,0:T(8,128)(4,1)S(1)} %constant_dynamic-slice_fusion.6, bf16[256,2,8,128]{3,0,2,1:T(8,128)(2,1)S(1)} %get-tuple-element.267, bf16[8,1,2,128,128]{4,3,2,1,0:T(8,128)(2,1)S(1)} %get-tuple-element.231), kind=kOutput, calls=%fused_computation.4.clone.1 | convolution fusion | flops 1086320640 | bytes 18367488 | tf_op jit(solution)/shard_map/while/body/eval_jaxpr/tkgd,nkpd->kgtnp/dot_general | solution.py:95
  156.0 4.4 %fusion.64 = f32[2,8,256]{2,1,0:T(8,128)S(1)} fusion(f32[2,8,128,256,8]{3,2,4,1,0:T(8,128)S(1)} %get-tuple-element.233, f32[2,8,256]{2,1,0:T(8,128)S(1)} %max.20, pred[8,128]{1,0:T(8,128)(4,1)S(1)} %constant_dynamic-slice_fusion.6), kind=kLoop, calls=%fused_computation.9.clone.1 | loop fusion | flops 20967424 | bytes 16811008 | tf_op jit(solution)/shard_map/while/body/eval_jaxpr/reduce_sum | solution.py:61
  160.4 6.4 %bitcast_add_fusion.2 = f32[2,8,256,128]{3,2,1,0:T(8,128)S(1)} fusion(f32[2,8,256,128]{3,2,1,0:T(8,128)S(1)} %get-tuple-element.252, f32[2,8,128,256,8]{3,2,4,1,0:T(8,128)S(1)} %get-tuple-element.233, f32[2,8,256]{2,1,0:T(8,128)S(1)} %max.20, pred[8,128]{1,0:T(8,128)(4,1)S(1)} %constant_dynamic-slice_fusion.6, ...), kind=kOutput, calls=%fused_computation.13.clone.1 | convolution fusion | flops 1095761920 | bytes 21529600 | tf_op jit(solution)/shard_map/while/body/eval_jaxpr/kgtnp,nkpd->kgtd/dot_general | solution.py:102
  168.2 2.5 %bitcast_reduce_fusion.2 = (f32[2,8,256]{2,1,0:T(8,128)S(1)}, f32[2,8,128,256,8]{3,2,4,1,0:T(8,128)S(1)}) fusion(pred[8,128]{1,0:T(8,128)(4,1)S(1)} %constant_dynamic-slice_fusion.6, bf16[256,2,8,128]{3,0,2,1:T(8,128)(2,1)S(1)} %get-tuple-element.267, bf16[8,1,2,128,128]{4,3,2,1,0:T(8,128)(2,1)S(1)} %get-tuple-element.231), kind=kOutput, calls=%fused_computation.4.clone.1 | convolution fusion | flops 1086320640 | bytes 18367488 | tf_op jit(solution)/shard_map/while/body/eval_jaxpr/tkgd,nkpd->kgtnp/dot_general | solution.py:95
  170.8 4.4 %fusion.64 = f32[2,8,256]{2,1,0:T(8,128)S(1)} fusion(f32[2,8,128,256,8]{3,2,4,1,0:T(8,128)S(1)} %get-tuple-element.233, f32[2,8,256]{2,1,0:T(8,128)S(1)} %max.20, pred[8,128]{1,0:T(8,128)(4,1)S(1)} %constant_dynamic-slice_fusion.6), kind=kLoop, calls=%fused_computation.9.clone.1 | loop fusion | flops 20967424 | bytes 16811008 | tf_op jit(solution)/shard_map/while/body/eval_jaxpr/reduce_sum | solution.py:61
  175.2 6.4 %bitcast_add_fusion.2 = f32[2,8,256,128]{3,2,1,0:T(8,128)S(1)} fusion(f32[2,8,256,128]{3,2,1,0:T(8,128)S(1)} %get-tuple-element.252, f32[2,8,128,256,8]{3,2,4,1,0:T(8,128)S(1)} %get-tuple-element.233, f32[2,8,256]{2,1,0:T(8,128)S(1)} %max.20, pred[8,128]{1,0:T(8,128)(4,1)S(1)} %constant_dynamic-slice_fusion.6, ...), kind=kOutput, calls=%fused_computation.13.clone.1 | convolution fusion | flops 1095761920 | bytes 21529600 | tf_op jit(solution)/shard_map/while/body/eval_jaxpr/kgtnp,nkpd->kgtd/dot_general | solution.py:102
  186.1 10.1 %collective-permute-done.2 = bf16[2,8,128]{2,1,0:T(8,128)(2,1)S(1)} collective-permute-done((bf16[2,8,128]{2,1,0:T(8,128)(2,1)S(1)}, bf16[2,8,128]{2,1,0:T(8,128)(2,1)S(1)}, u32[]{:S(2)}, u32[]{:S(2)}) %collective-permute-start.2) | collective-permute-done | bytes 4128 | tf_op jit(solution)/shard_map/ppermute | solution.py:11
  (84 shorter events, 19.4 us)
Async XLA Ops:
  0.6 6.6 %copy-start.1 = (s32[4,64]{1,0:T(4,128)S(1)}, s32[4,64]{1,0:T(4,128)}, u32[]{:S(2)}) copy-start(s32[4,64]{1,0:T(4,128)} %param.11) | copy-start | bytes 3076
  0.6 6.0 %copy-start = (s32[4]{0:T(128)S(1)}, s32[4]{0:T(128)}, u32[]{:S(2)}) copy-start(s32[4]{0:T(128)} %param.12) | copy-start | bytes 52
  18.5 6.0 %copy-start.3 = (bf16[128,2,2,128]{3,2,1,0:T(2,128)(2,1)S(1)}, bf16[128,2,2,128]{3,2,1,0:T(2,128)(2,1)}, u32[]{:S(2)}) copy-start(bf16[128,2,2,128]{3,2,1,0:T(2,128)(2,1)} %param.9) | copy-start | bytes 393220
  18.5 8.1 %copy-start.2 = (bf16[128,16,128]{2,1,0:T(8,128)(2,1)S(1)}, bf16[128,16,128]{2,1,0:T(8,128)(2,1)}, u32[]{:S(2)}) copy-start(bf16[128,16,128]{2,1,0:T(8,128)(2,1)} %param.8) | copy-start | bytes 1572868
  18.5 11.3 %copy-start.4 = (s32[8]{0:T(128)S(1)}, s32[8]{0:T(128)}, u32[]{:S(2)}) copy-start(s32[8]{0:T(128)} %param.13) | copy-start | bytes 100
  18.6 99.3 %all-to-all-start = ((bf16[8,4,2,2,128,128]{5,4,1,3,2,0:T(8,128)(2,1)}), bf16[8,4,2,2,128,128]{5,4,1,3,2,0:T(8,128)(2,1)}, u32[]{:S(2)}, u32[]{:S(2)}) async-start(bf16[8,4,2,2,128,128]{5,4,1,3,2,0:T(8,128)(2,1)} %copy.63), calls=%async_computation | async-start | bytes 8388608 | tf_op jit(solution)/shard_map/all_to_all | solution.py:136
  24.6 38.9 %collective-permute-start = (bf16[128,2,2,128]{3,0,2,1:T(8,128)(2,1)S(1)}, bf16[128,2,2,128]{3,0,2,1:T(8,128)(2,1)S(1)}, u32[]{:S(2)}, u32[]{:S(2)}) collective-permute-start(bf16[128,2,2,128]{3,0,2,1:T(8,128)(2,1)S(1)} %copy.55), channel_id=1, source_target_pairs={{0,2},{2,0},{4,6},{6,4},{8,10},{10,8},{12,14},{14,12},{1,3},{3,1},... | collective-permute-start | bytes 393224 | tf_op jit(solution)/shard_map/ppermute | solution.py:11
  26.6 49.4 %collective-permute-start.1 = (bf16[128,16,128]{2,1,0:T(8,128)(2,1)S(1)}, bf16[128,16,128]{2,1,0:T(8,128)(2,1)S(1)}, u32[]{:S(2)}, u32[]{:S(2)}) collective-permute-start(bf16[128,16,128]{2,1,0:T(8,128)(2,1)S(1)} %copy-done.2), channel_id=1, source_target_pairs={{0,2},{2,0},{4,6},{6,4},{8,10},{10,8},{12,14},{14,12},{1,3},{3,1},... | collective-permute-start | bytes 1572872 | tf_op jit(solution)/shard_map/ppermute | solution.py:11
  181.7 4.4 %collective-permute-start.4 = (bf16[2,8,128]{2,1,0:T(8,128)(2,1)S(1)}, bf16[2,8,128]{2,1,0:T(8,128)(2,1)S(1)}, u32[]{:S(2)}, u32[]{:S(2)}) collective-permute-start(bf16[2,8,128]{2,1,0:T(8,128)(2,1)S(1)} %dynamic-slice_convert_fusion.1), channel_id=1, source_target_pairs={{0,2},{2,0},{4,6},{6,4},{8,10},{10,8},{12,14},{14,12},{1,3},{3,1},... | collective-permute-start | bytes 12296 | tf_op jit(solution)/shard_map/ppermute | solution.py:11
  183.3 12.8 %collective-permute-start.3 = (bf16[2,8,128,128]{3,2,1,0:T(8,128)(2,1)S(1)}, bf16[2,8,128,128]{3,2,1,0:T(8,128)(2,1)S(1)}, u32[]{:S(2)}, u32[]{:S(2)}) collective-permute-start(bf16[2,8,128,128]{3,2,1,0:T(8,128)(2,1)S(1)} %dynamic-slice_convert_fusion), channel_id=1, source_target_pairs={{0,2},{2,0},{4,6},{6,4},{8,10},{10,8},{12,14},{14,12},{1,3},{3,1},... | collective-permute-start | bytes 1572872 | tf_op jit(solution)/shard_map/ppermute | solution.py:11
  183.9 12.2 %collective-permute-start.2 = (bf16[2,8,128]{2,1,0:T(8,128)(2,1)S(1)}, bf16[2,8,128]{2,1,0:T(8,128)(2,1)S(1)}, u32[]{:S(2)}, u32[]{:S(2)}) collective-permute-start(bf16[2,8,128]{2,1,0:T(8,128)(2,1)S(1)} %dynamic-slice_convert_fusion.2), channel_id=1, source_target_pairs={{0,2},{2,0},{4,6},{6,4},{8,10},{10,8},{12,14},{14,12},{1,3},{3,1},... | collective-permute-start | bytes 12296 | tf_op jit(solution)/shard_map/ppermute | solution.py:11
where the time goes:
time: 200 us; the launch traced here: 198 us
  waiting for transfers between devices  92.6 us (46%)
  matrix products  38.2 us (19%)
  local copies, waits for them, and re-layouts  31 us (16%)
  other arithmetic  22.3 us (11%)
  starting transfers between devices  11.8 us (6%)
  between operations  2.14 us (1%)
    ppermute x5, waiting for transfers between devices, swapped(): lax.ppermute(array, axis, [(i, i ^ 1 << apart) for i in range(lax.axis_si...  54.8 us
    all_to_all x1, waiting for transfers between devices, on_device(): lax.all_to_all(buffer, 'pool', split_axis=0, concat_axis=0, tiled=True)  37.8 us
    dot_general x4, matrix products, carry_values(): jnp.einsum('kgtnp,nkpd->kgtd', shaped, page_block[:, 1], preferred_elemen...  25.7 us
    reduce_sum x5, other arithmetic, update(): total_new = total_old * factor + jnp.sum(weights, axis=-1)  18.8 us
    dot_general x4, matrix products, turn(): jnp.einsum('tkgd,nkpd->kgtnp', query_heads, page_block[:, 0], preferred_e...  10.1 us
    gather x2, local copies, waits for them, and re-layouts, prepare(): buffer = pool[send_slots]  9.98 us
    unnamed x13, local copies, waits for them, and re-layouts  6.1 us
    all_to_all x1, starting transfers between devices, on_device(): lax.all_to_all(buffer, 'pool', split_axis=0, concat_axis=0, tiled=True)  5.97 us
  transfers between devices with their start and end apart: 6, of which 4 were waited for; matrix products, arithmetic and copies ran while one was open for 4% of the time, Pallas kernels for 0%

commit v1 on v0

v1 whole, which is shorter than its diff:
```python
import functools
import math

import jax
import jax.numpy as jnp
import numpy as np
from jax import lax
from jax.experimental import pallas as pl
from jax.experimental.pallas import tpu as pltpu
from jax.sharding import PartitionSpec as P

neg_big = -1e30
vmem_bytes = 32 * 1024 * 1024


def permuted(array, apart):
    return lax.ppermute(array, "pool", [(i, i ^ apart) for i in range(lax.axis_size("pool"))])


def half_of(ids):
    return 1 - (ids % 2 ^ ids // 2 % 2)


def select_pages(rows, page_count, holder, first_rank, take, slot_count):
    width = rows.shape[1]
    column = jnp.arange(width, dtype=jnp.int32)
    owned = (
        (rows >= holder[:, None] * slot_count)
        & (rows < (holder[:, None] + 1) * slot_count)
        & (column[None, :] < page_count[:, None])
    )
    before = column[None, :, None] > column[None, None, :]
    rank = jnp.sum((owned[:, None, :] & before).astype(jnp.int32), axis=-1)
    wanted = first_rank[:, None] + 2 * jnp.arange(take, dtype=jnp.int32)[None, :]
    matched = owned[:, None, :] & (rank[:, None, :] == wanted[:, :, None])
    present = jnp.any(matched, axis=-1)
    chosen = jnp.sum(jnp.where(matched, column[None, None, :], 0), axis=-1)
    local = rows - holder[:, None] * slot_count
    slot_id = jnp.sum(jnp.where(matched, local[:, None, :], 0), axis=-1)
    return chosen, slot_id, present


def gather_kernel(slots_ref, pool_ref, out_ref, sems):
    for i in range(out_ref.shape[0]):
        pltpu.make_async_copy(pool_ref.at[slots_ref[i]], out_ref.at[i], sems.at[i]).start()
    for i in range(out_ref.shape[0]):
        pltpu.make_async_copy(pool_ref.at[slots_ref[i]], out_ref.at[i], sems.at[i]).wait()


def gather_pages(pool, slots):
    count = slots.shape[0]
    return pl.pallas_call(
        gather_kernel,
        out_shape=jax.ShapeDtypeStruct((count, *pool.shape[1:]), pool.dtype),
        in_specs=[pl.BlockSpec(memory_space=pltpu.SMEM), pl.BlockSpec(memory_space=pl.ANY)],
        out_specs=pl.BlockSpec(memory_space=pl.ANY),
        scratch_shapes=[pltpu.SemaphoreType.DMA((count,))],
        name="gather_pages",
    )(slots, pool)


def attend_kernel(with_recent, chunk, group, valid_ref, *refs):
    if with_recent:
        q_a, q_b, pages, recent = refs[:4]
        refs = refs[4:]
    else:
        q_a, q_b, pages = refs[:3]
        refs = refs[3:]
    o_a, o_b, lse_a, lse_b, m_ref, l_ref, acc_ref = refs
    n_pages, _, _, page_len, head_dim = pages.shape
    rows = q_a.shape[1]
    factor = head_dim ** (-0.5) * math.log2(math.e)
    sides = (q_a, q_b)
    m_ref[...] = jnp.full_like(m_ref, neg_big)
    l_ref[...] = jnp.zeros_like(l_ref)
    acc_ref[...] = jnp.zeros_like(acc_ref)

    def step(keys, values, masks):
        scores = [
            lax.dot_general(
                keys, q[0], (((1,), (1,)), ((), ())), preferred_element_type=jnp.float32
            )
            for q in sides
        ]
        for side in range(2):
            s = scores[side]
            if masks is not None:
                s = jnp.where(masks[side], s, 2 * neg_big)
            m_old = m_ref[side]
            m_new = jnp.maximum(m_old, jnp.max(s, axis=0, keepdims=True))
            p = jnp.exp2((s - m_new) * factor)
            alpha = jnp.exp2((m_old - m_new) * factor)
            m_ref[side] = m_new
            l_ref[side] = l_ref[side] * alpha + jnp.sum(p, axis=0, keepdims=True)
            acc_ref[side] = acc_ref[side] * alpha + lax.dot_general(
                values,
                p.astype(jnp.bfloat16),
                (((0,), (0,)), ((), ())),
                preferred_element_type=jnp.float32,
            )

    key_at = lax.broadcasted_iota(jnp.int32, (page_len, rows), 0)
    for begin in range(0, n_pages, chunk):
        counts = [valid_ref[begin + i] for i in range(chunk)]
        least = functools.reduce(jnp.minimum, counts)

        @pl.when(least == page_len)
        def whole():
            span = pl.ds(begin, chunk)
            step(
                pages[span, 0, 0].reshape(chunk * page_len, head_dim),
                pages[span, 1, 0].reshape(chunk * page_len, head_dim),
                None,
            )

        @pl.when(least < page_len)
        def parts():
            for i in range(chunk):

                @pl.when(counts[i] > 0)
                def part():
                    seen = key_at < counts[i]
                    step(pages[begin + i, 0, 0], pages[begin + i, 1, 0], (seen, seen))

    if with_recent:
        token = lax.broadcasted_iota(jnp.int32, (page_len, rows), 1) + pl.program_id(1) * rows
        own_seen = key_at * group <= token
        other_seen = key_at < valid_ref[n_pages]
        step(recent[0, 0, 0], recent[0, 1, 0], (own_seen, other_seen))

    for side, (o_ref, lse_ref) in enumerate(((o_a, lse_a), (o_b, lse_b))):
        total = jnp.maximum(l_ref[side], 1e-30)
        o_ref[0] = (acc_ref[side] / total).astype(o_ref.dtype)
        lse_ref[0] = m_ref[side] * factor + jnp.log2(total)


def attend(valid, q_a, q_b, pages, recent, group):
    kv_heads, n_rows, head_dim = q_a.shape
    n_pages, _, _, page_len, _ = pages.shape
    rows = math.gcd(n_rows, 256)
    chunk = math.gcd(n_pages, 4)
    q_spec = pl.BlockSpec((1, rows, head_dim), lambda k, b: (k, b, 0))
    page_block = lambda count: pl.BlockSpec(
        (count, 2, 1, page_len, head_dim), lambda k, b: (0, 0, k, 0, 0)
    )
    o_spec = pl.BlockSpec((1, head_dim, rows), lambda k, b: (k, 0, b))
    lse_spec = pl.BlockSpec((1, 1, rows), lambda k, b: (k, 0, b))
    o_shape = jax.ShapeDtypeStruct((kv_heads, head_dim, n_rows), jnp.bfloat16)
    lse_shape = jax.ShapeDtypeStruct((kv_heads, 1, n_rows), jnp.float32)
    operands = (valid, q_a, q_b, pages) + (() if recent is None else (recent,))
    work = kv_heads * 2 * n_rows * n_pages * page_len
    return pl.pallas_call(
        functools.partial(attend_kernel, recent is not None, chunk, group),
        grid=(kv_heads, n_rows // rows),
        out_shape=(o_shape, o_shape, lse_shape, lse_shape),
        in_specs=[pl.BlockSpec(memory_space=pltpu.SMEM), q_spec, q_spec, page_block(n_pages)]
        + ([] if recent is None else [page_block(1)]),
        out_specs=(o_spec, o_spec, lse_spec, lse_spec),
        scratch_shapes=[
            pltpu.VMEM((2, 1, rows), jnp.float32),
            pltpu.VMEM((2, 1, rows), jnp.float32),
            pltpu.VMEM((2, head_dim, rows), jnp.float32),
        ],
        compiler_params=pltpu.CompilerParams(vmem_limit_bytes=vmem_bytes),
        cost_estimate=pl.CostEstimate(
            flops=4 * work * head_dim, bytes_accessed=6 * 2**20, transcendentals=work
        ),
        name="attend_far" if recent is None else "attend_near",
    )(*operands)


def combine(parts):
    top = functools.reduce(jnp.maximum, [lse for _, lse in parts])
    weights = [jnp.exp2(lse - top) for _, lse in parts]
    total = functools.reduce(jnp.add, weights)
    mixed = functools.reduce(
        jnp.add, [o.astype(jnp.float32) * w for (o, _), w in zip(parts, weights)]
    )
    return mixed / total, top + jnp.log2(total)


def merge_kernel(group, *refs):
    out_ref = refs[-1]
    parts = [(refs[2 * i], refs[2 * i + 1]) for i in range(len(refs) // 2)]
    tokens = out_ref.shape[0]
    heads = []
    for k in range(parts[0][0].shape[0]):
        mixed, _ = combine([(o[k], lse[k]) for o, lse in parts])
        heads.append(mixed.T.reshape(tokens, group, mixed.shape[0]))
    out_ref[...] = jnp.concatenate(heads, axis=1).astype(out_ref.dtype)


def on_device(queries, new_kv, pool, block_table, prefix_len, new_slots):
    owners = lax.axis_size("pool")
    half_count = owners // 2
    me = lax.axis_index("pool")
    slot_count, _, kv_heads, page_len, head_dim = pool.shape
    tokens, q_heads, _ = queries.shape
    group = q_heads // kv_heads
    take = block_table.shape[1] // owners // 2
    n_pages = half_count * take
    my_half = me // half_count
    far_half = 1 - my_half

    q_own = queries.reshape(tokens, kv_heads, group, head_dim).transpose(1, 0, 2, 3)
    q_own = q_own.reshape(kv_heads, tokens * group, head_dim)
    q_far = permuted(q_own, half_count)
    q_pair = permuted(q_own, 1)
    q_far_pair = permuted(q_far, 1)

    page_count = (prefix_len + page_len - 1) // page_len
    targets = np.arange(owners, dtype=np.int32)
    first = jnp.asarray(half_of(targets))
    _, send_slots, _ = select_pages(
        jnp.repeat(block_table, 2, axis=0),
        jnp.repeat(page_count, 2, axis=0),
        jnp.full((owners,), me, jnp.int32),
        first,
        take,
        slot_count,
    )
    groups = [list(range(half_count)), list(range(half_count, owners))]

    def exchange(which):
        slots = lax.dynamic_slice_in_dim(send_slots, which * half_count, half_count, 0)
        sent = gather_pages(pool, slots.reshape(-1))
        return lax.all_to_all(
            sent, "pool", split_axis=0, concat_axis=0, tiled=True, axis_index_groups=groups
        )

    pages_far = exchange(far_half)
    pages_near = exchange(my_half)

    holders = my_half * half_count + jnp.arange(half_count, dtype=jnp.int32)

    def valid_keys(device):
        row = lax.dynamic_slice_in_dim(block_table, device // 2, 1, 0)
        length = lax.dynamic_slice_in_dim(prefix_len, device // 2, 1, 0)
        chosen, _, present = select_pages(
            jnp.broadcast_to(row, (half_count, row.shape[1])),
            jnp.broadcast_to((length + page_len - 1) // page_len, (half_count,)),
            holders,
            jnp.broadcast_to(half_of(device), (half_count,)),
            take,
            slot_count,
        )
        left = jnp.clip(length[:, None] - chosen * page_len, 0, page_len)
        return jnp.where(present, left, 0).reshape(-1)

    valid_far = valid_keys(me ^ half_count)
    other_limit = ((1 - half_of(me)) * page_len).reshape(1).astype(jnp.int32)
    valid_near = jnp.concatenate([valid_keys(me), other_limit])

    new_page = new_kv.transpose(1, 2, 0, 3)[None]
    o_far, o_far_pair, lse_far, lse_far_pair = attend(
        valid_far, q_far, q_far_pair, pages_far, None, group
    )
    back_o, back_lse = permuted(o_far_pair, 1), permuted(lse_far_pair, 1)
    far_o, far_lse = combine([(o_far, lse_far), (back_o, back_lse)])
    home_o = permuted(far_o.astype(jnp.bfloat16), half_count)
    home_lse = permuted(far_lse, half_count)

    o_near, o_pair, lse_near, lse_pair = attend(
        valid_near, q_own, q_pair, pages_near, new_page, group
    )
    pair_o, pair_lse = permuted(o_pair, 1), permuted(lse_pair, 1)
    attended = pl.pallas_call(
        functools.partial(merge_kernel, group),
        out_shape=jax.ShapeDtypeStruct(queries.shape, queries.dtype),
        compiler_params=pltpu.CompilerParams(vmem_limit_bytes=vmem_bytes),
        name="merge",
    )(o_near, lse_near, pair_o, pair_lse, home_o, home_lse)

    own_slot = lax.dynamic_index_in_dim(new_slots, me, 0, keepdims=False)
    updated_pool = lax.dynamic_update_slice_in_dim(pool, new_page, own_slot % slot_count, 0)
    return attended, updated_pool


def solution(mesh):
    placed = (
        P(("groups", "pool"), "head", None),
        P(("groups", "pool"), None, "head", None),
        P(("groups", "pool"), None, "head", None, None),
        P("groups", None),
        P("groups"),
        P("groups"),
    )
    return jax.shard_map(
        on_device,
        mesh=mesh,
        in_specs=placed,
        out_specs=(
            P(("groups", "pool"), "head", None),
            P(("groups", "pool"), None, "head", None, None),
        ),
        check_vma=False,
    )
```

time: 200 us -> 301 us (1.50)
  Pallas kernels: 0 us -> 201 us
  waiting for transfers between devices: 92.6 us -> 51.5 us
  matrix products: 38.2 us -> 0 us
  other arithmetic: 22.3 us -> 4.54 us
  local copies, waits for them, and re-layouts: 31 us -> 16.5 us
  starting transfers between devices: 11.8 us -> 21.4 us
    pallas_call x0 -> x5, Pallas kernels: none -> 201 us  [the longest x2 131 us: gather_pages(): pl.pallas_call(gather_kernel, out_shape=jax.ShapeDtypeStruct((count, *poo...]
    dot_general x10 -> x0, matrix products: 38.2 us -> none  [the longest x4 25.7 us: carry_values(): jnp.einsum('kgtnp,nkpd->kgtd', shaped, page_block[:, 1], preferred_elemen...]
    all_to_all x1 -> x2, waiting for transfers between devices: 37.8 us -> 0.01 us  [exchange(): lax.all_to_all(sent, 'pool', split_axis=0, concat_axis=0, tiled=True, axi...]
    reduce_sum x6 -> x3, other arithmetic: 19 us -> 0.66 us  [the longest x2 0.44 us: select_pages(): rank = jnp.sum((owned[:, None, :] & before).astype(jnp.int32), axis=-1)]
    gather x4 -> x0, local copies, waits for them, and re-layouts: 11.2 us -> none  [the longest x2 9.98 us: prepare(): buffer = pool[send_slots]]
    ppermute x5 -> x9, starting transfers between devices: 5.79 us -> 13.4 us  [permuted(): lax.ppermute(array, 'pool', [(i, i ^ apart) for i in range(lax.axis_size(...]
    unnamed x13 -> x29, local copies, waits for them, and re-layouts: 6.1 us -> 11.9 us
    slice x4 -> x0, local copies, waits for them, and re-layouts: 5.24 us -> none  [carry_values(): page_block[:, 1]]
  transfers between devices with their start and end apart: 6 -> 11, of which waited for: 4 -> 4; matrix products, arithmetic and copies ran while one was open for 4% -> 3% of each run, Pallas kernels for 0% -> 45%
where the time goes in v1:
time: 301 us; the launch traced here: 298 us
  Pallas kernels  201 us (67%)
  waiting for transfers between devices  51.5 us (17%)
  starting transfers between devices  21.4 us (7%)
  local copies, waits for them, and re-layouts  16.5 us (5%)
  other arithmetic  4.54 us (2%)
    pallas_call x2, Pallas kernels, gather_pages(): pl.pallas_call(gather_kernel, out_shape=jax.ShapeDtypeStruct((count, *poo...  131 us
    pallas_call x2, Pallas kernels, attend(): pl.pallas_call(functools.partial(attend_kernel, recent is not None, chunk...  68.9 us
    ppermute x9, waiting for transfers between devices, permuted(): lax.ppermute(array, 'pool', [(i, i ^ apart) for i in range(lax.axis_size(...  51.5 us
    ppermute x9, starting transfers between devices, permuted(): lax.ppermute(array, 'pool', [(i, i ^ apart) for i in range(lax.axis_size(...  13.4 us
    unnamed x29, local copies, waits for them, and re-layouts  11.9 us
    all_to_all x2, starting transfers between devices, exchange(): lax.all_to_all(sent, 'pool', split_axis=0, concat_axis=0, tiled=True, axi...  8.01 us
  transfers between devices with their start and end apart: 11, of which 4 were waited for; matrix products, arithmetic and copies ran while one was open for 3% of the time, Pallas kernels for 45%

profile of v1, /device:TPU:2, one launch (start us, length us, event | category | flops | bytes accessed | tf_op | source)
XLA Modules:
  0.0 297.8 jit_solution(11222029248819397009)
XLA Ops:
  0.7 6.0 %copy.33.pool_ref = bf16[33,2,2,128,128]{4,3,2,1,0:T(8,128)(2,1)} copy(bf16[33,2,2,128,128]{4,3,2,1,0:T(8,128)(2,1)} %param.9) | data formatting | bytes 8650752
  8.3 65.4 %gather_pages.3 = bf16[16,2,2,128,128]{4,3,2,1,0:T(8,128)(2,1)} custom-call(s32[16]{0:T(128)} %reshape.295.slots_ref, bf16[33,2,2,128,128]{4,3,2,1,0:T(8,128)(2,1)} %copy.33.pool_ref), custom_call_target="tpu_custom_call" | custom-call | tf_op jit(solution)/shard_map/gather_pages/pallas_call | solution.py:52
  73.7 3.8 %all-to-all-start.1 = ((bf16[16,2,2,128,128]{4,3,2,1,0:T(8,128)(2,1)}), bf16[16,2,2,128,128]{4,3,2,1,0:T(8,128)(2,1)S(1)}, u32[]{:S(2)}, u32[]{:S(2)}) async-start(bf16[16,2,2,128,128]{4,3,2,1,0:T(8,128)(2,1)} %gather_pages.3), calls=%async_computation.1 | async-start | bytes 4194304 | tf_op jit(solution)/shard_map/all_to_all | solution.py:227
  78.2 65.4 %gather_pages.2 = bf16[16,2,2,128,128]{4,3,2,1,0:T(8,128)(2,1)} custom-call(s32[16]{0:T(128)} %reshape.294.slots_ref, bf16[33,2,2,128,128]{4,3,2,1,0:T(8,128)(2,1)} %copy.33.pool_ref), custom_call_target="tpu_custom_call" | custom-call | tf_op jit(solution)/shard_map/gather_pages/pallas_call | solution.py:52
  143.7 1.3 copy-done.1
  145.0 4.2 %all-to-all-start = ((bf16[16,2,2,128,128]{4,3,2,1,0:T(8,128)(2,1)}), bf16[16,2,2,128,128]{4,3,2,1,0:T(8,128)(2,1)S(1)}, u32[]{:S(2)}, u32[]{:S(2)}) async-start(bf16[16,2,2,128,128]{4,3,2,1,0:T(8,128)(2,1)} %gather_pages.2), calls=%async_computation | async-start | bytes 4194304 | tf_op jit(solution)/shard_map/all_to_all | solution.py:227
  149.2 0.8 copy_bitcast_fusion.refs_0_
  150.1 2.6 collective-permute-start.3
  152.6 2.0 collective-permute-start
  157.9 24.8 %collective-permute-done.3.refs_0_ = bf16[2,1024,128]{2,1,0:T(8,128)(2,1)S(1)} collective-permute-done((bf16[2,1024,128]{2,1,0:T(8,128)(2,1)}, bf16[2,1024,128]{2,1,0:T(8,128)(2,1)S(1)}, u32[]{:S(2)}, u32[]{:S(2)}) %collective-permute-start.3) | collective-permute-done | bytes 524320 | tf_op jit(solution)/shard_map/ppermute | solution.py:17
  182.7 1.7 collective-permute-start.4
  186.9 9.3 %collective-permute-done.4.refs_1_ = bf16[2,1024,128]{2,1,0:T(8,128)(2,1)} collective-permute-done((bf16[2,1024,128]{2,1,0:T(8,128)(2,1)S(1)}, bf16[2,1024,128]{2,1,0:T(8,128)(2,1)}, u32[]{:S(2)}, u32[]{:S(2)}) %collective-permute-start.4) | collective-permute-done | bytes 524320 | tf_op jit(solution)/shard_map/ppermute | solution.py:17
  196.1 1.6 copy-done.2
  197.7 1.0 copy-done.6
  198.8 41.8 %attend_far.1 = (bf16[2,128,1024]{2,1,0:T(8,128)(2,1)S(1)}, bf16[2,128,1024]{2,1,0:T(8,128)(2,1)}, f32[2,1,1024]{2,1,0:T(1,128)S(1)}, f32[2,1,1024]{2,1,0:T(1,128)S(1)}) custom-call(s32[16]{0:T(128)S(1)} %select_n.127.valid_ref, bf16[2,1024,128]{2,1,0:T(8,128)(2,1)S(1)} %copy-done.6, bf16[2,1024,128]{2,1,0:T(8,128)(2,1)} %collective-permute-done.4.refs_1_, ...), custom_call_target="tpu_custom_call" | custom-call | flops 4294967296 | bytes 6291456 | tf_op jit(solution)/shard_map/attend_far/pallas_call | solution.py:152
  240.6 2.0 collective-permute-start.6
  242.6 27.1 %attend_near.1 = (bf16[2,128,1024]{2,1,0:T(8,128)(2,1)S(1)}, bf16[2,128,1024]{2,1,0:T(8,128)(2,1)}, f32[2,1,1024]{2,1,0:T(1,128)S(1)}, f32[2,1,1024]{2,1,0:T(1,128)S(1)}) custom-call(s32[17]{0:T(128)S(1)} %pad_add_fusion.valid_ref, bf16[2,1024,128]{2,1,0:T(8,128)(2,1)} %copy_bitcast_fusion.refs_0_, bf16[2,1024,128]{2,1,0:T(8,128)(2,1)} %collective-permute-done.refs_1_, ...), custom_call_target="tpu_custom_call" | custom-call | flops 4294967296 | bytes 6291456 | tf_op jit(solution)/shard_map/attend_near/pallas_call | solution.py:152
  269.8 1.3 divide_convert_fusion
  271.2 2.8 collective-permute-start.7
  275.2 2.0 collective-permute-start.2
  278.1 3.8 %collective-permute-done.2.refs_3_ = f32[2,1,1024]{2,1,0:T(1,128)S(1)} collective-permute-done((f32[2,1,1024]{2,1,0:T(1,128)S(1)}, f32[2,1,1024]{2,1,0:T(1,128)S(1)}, u32[]{:S(2)}, u32[]{:S(2)}) %collective-permute-start.2) | collective-permute-done | bytes 8224 | tf_op jit(solution)/shard_map/ppermute | solution.py:17
  281.9 13.6 %collective-permute-done.8.refs_5_ = f32[2,1,1024]{2,1,0:T(1,128)S(1)} collective-permute-done((f32[2,1,1024]{2,1,0:T(1,128)S(1)}, f32[2,1,1024]{2,1,0:T(1,128)S(1)}, u32[]{:S(2)}, u32[]{:S(2)}) %collective-permute-start.8) | collective-permute-done | bytes 8224 | tf_op jit(solution)/shard_map/ppermute | solution.py:17
  295.5 1.0 copy-done.4
  296.6 1.2 merge.1
  (73 shorter events, 8.2 us)
Async XLA Ops:
  0.6 148.6 %copy-start = (bf16[128,16,128]{2,1,0:T(8,128)(2,1)S(1)}, bf16[128,16,128]{2,1,0:T(8,128)(2,1)}, u32[]{:S(2)}) copy-start(bf16[128,16,128]{2,1,0:T(8,128)(2,1)} %param.7) | copy-start | bytes 1572868
  0.6 6.6 %copy-start.10 = (s32[8]{0:T(128)S(1)}, s32[8]{0:T(128)}, u32[]{:S(2)}) copy-start(s32[8]{0:T(128)} %constant.160.clone) | copy-start | bytes 100
  0.7 6.0 %copy-start.8 = (s32[4,64]{1,0:T(4,128)S(1)}, s32[4,64]{1,0:T(4,128)}, u32[]{:S(2)}) copy-start(s32[4,64]{1,0:T(4,128)} %param.10) | copy-start | bytes 3076
  0.7 6.1 %copy-start.9 = (s32[4]{0:T(128)S(1)}, s32[4]{0:T(128)}, u32[]{:S(2)}) copy-start(s32[4]{0:T(128)} %param.11) | copy-start | bytes 52
  73.7 70.0 %all-to-all-start.1 = ((bf16[16,2,2,128,128]{4,3,2,1,0:T(8,128)(2,1)}), bf16[16,2,2,128,128]{4,3,2,1,0:T(8,128)(2,1)S(1)}, u32[]{:S(2)}, u32[]{:S(2)}) async-start(bf16[16,2,2,128,128]{4,3,2,1,0:T(8,128)(2,1)} %gather_pages.3), calls=%async_computation.1 | async-start | bytes 4194304 | tf_op jit(solution)/shard_map/all_to_all | solution.py:227
  143.7 43.1 %copy-start.7 = (bf16[128,2,2,128]{3,2,1,0:T(2,128)(2,1)S(1)}, bf16[128,2,2,128]{3,2,1,0:T(2,128)(2,1)}, u32[]{:S(2)}) copy-start(bf16[128,2,2,128]{3,2,1,0:T(2,128)(2,1)} %param.8) | copy-start | bytes 393220
  143.7 1.3 copy-start.1
  145.0 97.6 %all-to-all-start = ((bf16[16,2,2,128,128]{4,3,2,1,0:T(8,128)(2,1)}), bf16[16,2,2,128,128]{4,3,2,1,0:T(8,128)(2,1)S(1)}, u32[]{:S(2)}, u32[]{:S(2)}) async-start(bf16[16,2,2,128,128]{4,3,2,1,0:T(8,128)(2,1)} %gather_pages.2), calls=%async_computation | async-start | bytes 4194304 | tf_op jit(solution)/shard_map/all_to_all | solution.py:227
  150.1 32.7 %collective-permute-start.3 = (bf16[2,1024,128]{2,1,0:T(8,128)(2,1)}, bf16[2,1024,128]{2,1,0:T(8,128)(2,1)S(1)}, u32[]{:S(2)}, u32[]{:S(2)}) collective-permute-start(bf16[2,1024,128]{2,1,0:T(8,128)(2,1)} %copy_bitcast_fusion.refs_0_), channel_id=1, source_target_pairs={{0,8},{2,10},{4,12},{6,14},{8,0},{10,2},{12,4},{14,6},{1,9},{3,11}... | collective-permute-start | bytes 1572872 | tf_op jit(solution)/shard_map/ppermute | solution.py:17
  152.6 89.9 %collective-permute-start = (bf16[2,1024,128]{2,1,0:T(8,128)(2,1)}, bf16[2,1024,128]{2,1,0:T(8,128)(2,1)}, u32[]{:S(2)}, u32[]{:S(2)}) collective-permute-start(bf16[2,1024,128]{2,1,0:T(8,128)(2,1)} %copy_bitcast_fusion.refs_0_), channel_id=1, source_target_pairs={{0,2},{2,0},{4,6},{6,4},{8,10},{10,8},{12,14},{14,12},{1,3},{3,1},... | collective-permute-start | bytes 1572872 | tf_op jit(solution)/shard_map/ppermute | solution.py:17
  182.7 13.4 %collective-permute-start.4 = (bf16[2,1024,128]{2,1,0:T(8,128)(2,1)S(1)}, bf16[2,1024,128]{2,1,0:T(8,128)(2,1)}, u32[]{:S(2)}, u32[]{:S(2)}) collective-permute-start(bf16[2,1024,128]{2,1,0:T(8,128)(2,1)S(1)} %collective-permute-done.3.refs_0_), channel_id=1, source_target_pairs={{0,2},{2,0},{4,6},{6,4},{8,10},{10,8},{12,14},{14,12},{1,3},{3,1},... | collective-permute-start | bytes 1572872 | tf_op jit(solution)/shard_map/ppermute | solution.py:17
  184.5 0.8 copy-start.5
  196.1 1.6 copy-start.2
  197.7 1.0 copy-start.6
  240.6 29.2 %collective-permute-start.5 = (f32[2,1,1024]{2,1,0:T(1,128)S(1)}, f32[2,1,1024]{2,1,0:T(1,128)S(1)}, u32[]{:S(2)}, u32[]{:S(2)}) collective-permute-start(f32[2,1,1024]{2,1,0:T(1,128)S(1)} %get-tuple-element.16), channel_id=1, source_target_pairs={{0,2},{2,0},{4,6},{6,4},{8,10},{10,8},{12,14},{14,12},{1,3},{3,1},... | collective-permute-start | bytes 24584 | tf_op jit(solution)/shard_map/ppermute | solution.py:17
  240.6 29.2 %collective-permute-start.6 = (bf16[2,128,1024]{2,1,0:T(8,128)(2,1)}, bf16[2,128,1024]{2,1,0:T(8,128)(2,1)}, u32[]{:S(2)}, u32[]{:S(2)}) collective-permute-start(bf16[2,128,1024]{2,1,0:T(8,128)(2,1)} %get-tuple-element.17), channel_id=1, source_target_pairs={{0,2},{2,0},{4,6},{6,4},{8,10},{10,8},{12,14},{14,12},{1,3},{3,1},... | collective-permute-start | bytes 1572872 | tf_op jit(solution)/shard_map/ppermute | solution.py:17
  242.6 31.3 %copy-start.11 = (s32[8]{0:T(128)S(1)}, s32[8]{0:T(128)}, u32[]{:S(2)}) copy-start(s32[8]{0:T(128)} %param.12) | copy-start | bytes 100
  269.7 1.5 copy-start.3
  269.7 25.8 %collective-permute-start.1 = (bf16[2,128,1024]{2,1,0:T(8,128)(2,1)}, bf16[2,128,1024]{2,1,0:T(8,128)(2,1)S(1)}, u32[]{:S(2)}, u32[]{:S(2)}) collective-permute-start(bf16[2,128,1024]{2,1,0:T(8,128)(2,1)} %get-tuple-element.12), channel_id=1, source_target_pairs={{0,2},{2,0},{4,6},{6,4},{8,10},{10,8},{12,14},{14,12},{1,3},{3,1},... | collective-permute-start | bytes 1572872 | tf_op jit(solution)/shard_map/ppermute | solution.py:17
  271.2 24.4 %collective-permute-start.7 = (bf16[2,128,1024]{2,1,0:T(8,128)(2,1)S(1)}, bf16[2,128,1024]{2,1,0:T(8,128)(2,1)S(1)}, u32[]{:S(2)}, u32[]{:S(2)}) collective-permute-start(bf16[2,128,1024]{2,1,0:T(8,128)(2,1)S(1)} %divide_convert_fusion), channel_id=1, source_target_pairs={{0,8},{2,10},{4,12},{6,14},{8,0},{10,2},{12,4},{14,6},{1,9},{3,11}... | collective-permute-start | bytes 1572872 | tf_op jit(solution)/shard_map/ppermute | solution.py:17
  275.2 6.7 %collective-permute-start.2 = (f32[2,1,1024]{2,1,0:T(1,128)S(1)}, f32[2,1,1024]{2,1,0:T(1,128)S(1)}, u32[]{:S(2)}, u32[]{:S(2)}) collective-permute-start(f32[2,1,1024]{2,1,0:T(1,128)S(1)} %get-tuple-element.13), channel_id=1, source_target_pairs={{0,2},{2,0},{4,6},{6,4},{8,10},{10,8},{12,14},{14,12},{1,3},{3,1},... | collective-permute-start | bytes 24584 | tf_op jit(solution)/shard_map/ppermute | solution.py:17
  277.2 18.3 %collective-permute-start.8 = (f32[2,1,1024]{2,1,0:T(1,128)S(1)}, f32[2,1,1024]{2,1,0:T(1,128)S(1)}, u32[]{:S(2)}, u32[]{:S(2)}) collective-permute-start(f32[2,1,1024]{2,1,0:T(1,128)S(1)} %get-tuple-element.20), channel_id=1, source_target_pairs={{0,8},{2,10},{4,12},{6,14},{8,0},{10,2},{12,4},{14,6},{1,9},{3,11}... | collective-permute-start | bytes 24584 | tf_op jit(solution)/shard_map/ppermute | solution.py:17
  295.5 1.0 copy-start.4
